TPU v7x, 32 devices: a whole 2x2x4 slice. The times are simulated.
32 devices in a mesh: dp: 8 (over z, x), tensor: 4 (over y, core).
Axes of the slice: x: 2, y: 2, z: 4, core: 2. Of those that a mesh axis runs over, the one named last changes fastest.
Arguments:
- inputs: bfloat16 [8192, 6144], P('dp'), may hold values from -6 to 6
- pre_act: bfloat16 [8192, 1024], P('dp', 'tensor'), may hold values from -6 to 6
- grad_hidden: bfloat16 [8192, 1024], P('dp', 'tensor'), may hold values from -6 to 6
- master: float32 [6144, 1024], P('dp', 'tensor'), may hold values from -0.1875 to 0.1875
- moment_one: float32 [6144, 1024], P('dp', 'tensor'), may hold values from -6 to 6
- moment_two: float32 [6144, 1024], P('dp', 'tensor'), may hold values from 1 to 32768
Outputs:
- grad_input: bfloat16 [8192, 6144], P('dp', 'tensor')
- new_master: float32 [6144, 1024], P('dp', 'tensor')
- new_one: float32 [6144, 1024], P('dp', 'tensor')
- new_two: float32 [6144, 1024], P('dp', 'tensor')
- new_weights: bfloat16 [6144, 1024], P(None, 'tensor')
All inputs are finite; a program needn't handle non-finite values.
Results may differ from a plain program's by a relative error of at most 0.013.
Values may be sent and summed in bfloat16 or wider, within the bound.
A program may use at most 128 MiB of HBM per device.

v0:
```python
import math

import jax
import jax.numpy as jnp
from jax import lax
from jax.sharding import PartitionSpec as P

QBLOCK = 256
ADAM_STEP = 10


def gelu_slope(value):
    cdf = 0.5 * (1.0 + jax.scipy.special.erf(value / math.sqrt(2.0)))
    pdf = jnp.exp(-0.5 * value * value) / math.sqrt(2.0 * math.pi)
    return cdf + value * pdf


def encode(term):
    rows, cols = term.shape
    blocks = term.reshape(rows, cols // QBLOCK, QBLOCK)
    scale = (jnp.max(jnp.abs(blocks), axis=2) + 1e-06) / 127.0
    codes = jnp.clip(blocks / scale[:, :, None], -127.0, 127.0).astype(jnp.bfloat16)
    return (codes.reshape(rows, cols), scale)


def decode(codes, scale):
    rows, cols = codes.shape
    blocks = codes.astype(jnp.float32).reshape(rows, cols // QBLOCK, QBLOCK)
    return (blocks * scale[:, :, None]).reshape(rows, cols)


def local(inputs, pre_act, grad_hidden, master, moment_one, moment_two):
    act_grad = (grad_hidden.astype(jnp.float32) * gelu_slope(pre_act.astype(jnp.float32))).astype(
        jnp.bfloat16
    )
    weights = master.astype(jnp.bfloat16)
    terms = jnp.einsum(
        "th,dh->td",
        act_grad,
        lax.all_gather(weights, "dp", axis=0, tiled=True),
        preferred_element_type=jnp.float32,
    )
    grad_input = lax.psum_scatter(
        terms.astype(jnp.bfloat16), "tensor", scatter_dimension=1, tiled=True
    )
    term = jnp.einsum("tr,th->rh", inputs, act_grad, preferred_element_type=jnp.float32)
    codes, scale = encode(term)
    grad = lax.psum_scatter(decode(codes, scale), "dp", scatter_dimension=0, tiled=True)
    new_one = 0.9 * moment_one + 0.1 * grad
    new_two = 0.999 * moment_two + 0.001 * grad * grad
    corr_one = 1.0 - 0.9**ADAM_STEP
    corr_two = 1.0 - 0.999**ADAM_STEP
    update = new_one / corr_one / (jnp.sqrt(new_two / corr_two) + 1e-08) + 0.01 * master
    new_master = master - 0.01 * update
    new_weights = lax.all_gather(new_master.astype(jnp.bfloat16), "dp", axis=0, tiled=True)
    return (grad_input, new_master, new_one, new_two, new_weights)


def solution(mesh):
    in_specs = (
        P("dp", None),
        P("dp", "tensor"),
        P("dp", "tensor"),
        P("dp", "tensor"),
        P("dp", "tensor"),
        P("dp", "tensor"),
    )
    out_specs = (
        P("dp", "tensor"),
        P("dp", "tensor"),
        P("dp", "tensor"),
        P("dp", "tensor"),
        P(None, "tensor"),
    )
    return jax.shard_map(local, mesh=mesh, in_specs=in_specs, out_specs=out_specs, check_vma=False)
```

profile of v0, /device:TPU:0, one launch (start us, length us, event | category | flops | bytes accessed | tf_op | source)
XLA Modules:
  0.0 370.6 jit_solution(6185741115981934483)
XLA Ops:
  7.2 0.0 reduce-scatter.5.cloned.1.call-start
  7.2 7.5 %abs_reduce_fusion = (f32[6144]{0:T(1024)S(1)}, f32[256,6144]{1,0:T(8,128)S(1)}) fusion(bf16[1024,6144]{1,0:T(8,128)(2,1)} %param.6, bf16[1024,256]{1,0:T(8,128)(2,1)} %param.7, bf16[1024,256]{1,0:T(8,128)(2,1)} %param.8), kind=kOutput, calls=%fused_computation.3 | convolution fusion | flops 3227510784 | bytes 19947520 | tf_op jit(solution)/shard_map/tr,th->rh/dot_general | solution.py:46
  14.7 3.6 multiply_bitcast_fusion
  18.3 0.0 reduce-scatter.5.cloned.1.call-update
  18.3 0.0 all-gather.3.cloned.1.call-start
  18.4 1.1 copy-done
  19.4 0.8 convert_element_type.34
  20.2 0.0 all-gather.3.cloned.1.call-update
  20.2 0.0 all-gather.5.cloned.1.call-start
  20.3 0.3 copy.14
  20.5 1.1 copy.11
  21.7 1.1 copy.12
  22.9 116.3 %reduce-scatter.5.cloned.1.call-done = f32[768,256]{0,1:T(8,128)} async-done(((f32[6144,256]{0,1:T(8,128)}), f32[768,256]{0,1:T(8,128)}) %reduce-scatter.5.cloned.1.call-update) | async-done | bytes 786448 | tf_op jit(solution)/shard_map/reduce_scatter | solution.py:48
  139.1 3.0 fusion.12
  142.1 0.0 all-gather.5.cloned.1.call-update
  142.1 0.0 reduce-scatter.3.cloned.1.call-start
  142.2 59.3 %all-gather.3.cloned.1.call-done = bf16[6144,256]{1,0:T(8,128)(2,1)} async-done(((bf16[768,256]{1,0:T(8,128)(2,1)}), bf16[6144,256]{1,0:T(8,128)(2,1)}) %all-gather.3.cloned.1.call-update) | async-done | bytes 3145744 | tf_op jit(solution)/shard_map/all_gather | solution.py:40
  201.5 10.5 %convolution_convert_fusion = bf16[1024,6144]{1,0:T(8,128)(2,1)} fusion(bf16[6144,256]{1,0:T(8,128)(2,1)} %all-gather.3.cloned.1.call-done, bf16[1024,256]{1,0:T(8,128)(2,1)} %param.7, bf16[1024,256]{1,0:T(8,128)(2,1)} %param.8), kind=kOutput, calls=%fused_computation | convolution fusion | flops 3230662656 | bytes 16777216 | tf_op jit(solution)/shard_map/th,dh->td/dot_general | solution.py:37
  212.0 1.1 copy.15
  213.2 1.1 copy.16
  214.3 1.1 copy.17
  215.5 47.9 %all-gather.5.cloned.1.call-done = bf16[6144,256]{0,1:T(8,128)(2,1)} async-done(((bf16[768,256]{0,1:T(8,128)(2,1)}), bf16[6144,256]{0,1:T(8,128)(2,1)}) %all-gather.5.cloned.1.call-update) | async-done | bytes 3145744 | tf_op jit(solution)/shard_map/all_gather | solution.py:55
  263.4 4.6 %copy.18 = bf16[6144,256]{1,0:T(8,128)(2,1)} copy(bf16[6144,256]{0,1:T(8,128)(2,1)} %all-gather.5.cloned.1.call-done) | data formatting | bytes 6291456
  268.0 96.0 %reduce-scatter.3.cloned.1.call-done = bf16[1024,1536]{1,0:T(8,128)(2,1)} async-done(((bf16[1024,6144]{1,0:T(8,128)(2,1)}), bf16[1024,1536]{1,0:T(8,128)(2,1)}) %reduce-scatter.3.cloned.1.call-update) | async-done | bytes 3145744 | tf_op jit(solution)/shard_map/reduce_scatter | solution.py:43
  (7 shorter events, 0.0 us)
Async XLA Ops:
  7.2 132.0 %reduce-scatter.5.cloned.1.call-start = ((), (), s32[]{:S(2)}) async-start(), calls=%async_computation.4 | async-start | bytes 7077888 | tf_op jit(solution)/shard_map/reduce_scatter | solution.py:48
  18.3 1.1 copy-start
  18.3 2.3 copy-start.1
  18.3 3.4 copy-start.2
  18.3 183.2 %all-gather.3.cloned.1.call-start = ((), (), s32[]{:S(2)}) async-start(), calls=%async_computation.2 | async-start | bytes 3538944 | tf_op jit(solution)/shard_map/all_gather | solution.py:40
  20.2 243.2 %all-gather.5.cloned.1.call-start = ((), (), s32[]{:S(2)}) async-start(), calls=%async_computation.5 | async-start | bytes 3538944 | tf_op jit(solution)/shard_map/all_gather | solution.py:55
  142.1 221.9 %reduce-scatter.3.cloned.1.call-start = ((), (), s32[]{:S(2)}) async-start(), calls=%async_computation.3 | async-start | bytes 15728640 | tf_op jit(solution)/shard_map/reduce_scatter | solution.py:43
Sparse Core Ops, SparseCore 0:
  18.4 120.6 reduce-scatter.4
  141.9 59.5 all-gather.2
  204.3 59.0 all-gather.4
  266.4 97.5 reduce-scatter.2
where the time goes:
time: 371 us
  waiting for transfers between devices  320 us (86%)
  matrix products  18 us (5%)
  between operations  13.8 us (4%)
  local copies, waits for them, and re-layouts  11.7 us (3%)
  other arithmetic  7.34 us (2%)
    reduce_scatter x1, waiting for transfers between devices, local(): lax.psum_scatter(decode(codes, scale), 'dp', scatter_dimension=0, tiled=T...  116 us
    reduce_scatter x1, waiting for transfers between devices, local(): lax.psum_scatter(terms.astype(jnp.bfloat16), 'tensor', scatter_dimension=...  96 us
    all_gather x1, waiting for transfers between devices, local(): lax.all_gather(weights, 'dp', axis=0, tiled=True)  59.3 us
    all_gather x1, waiting for transfers between devices, local(): lax.all_gather(new_master.astype(jnp.bfloat16), 'dp', axis=0, tiled=True)  47.9 us
    unnamed x13, local copies, waits for them, and re-layouts  11.7 us
    dot_general x1, matrix products, local(): jnp.einsum('th,dh->td', act_grad, lax.all_gather(weights, 'dp', axis=0, t...  10.5 us
    dot_general x1, matrix products, local(): jnp.einsum('tr,th->rh', inputs, act_grad, preferred_element_type=jnp.floa...  7.46 us
  transfers between devices with their start and end apart: 4, of which 4 were waited for; matrix products, arithmetic and copies ran while one was open for 7% of the time, Pallas kernels for 0%

commit v1 on v0

v1 whole, which is shorter than its diff:
```python
import functools
import math

import jax
import jax.numpy as jnp
from jax import lax
from jax.experimental import pallas as pl
from jax.experimental.pallas import tpu as pltpu
from jax.sharding import PartitionSpec as P

QBLOCK = 256
ADAM_STEP = 10
Z, X, T = 4, 2, 4
W_SPLIT = 464
G_SPLIT = 160
N_SPLIT = 640
MESH = pl.DeviceIdType.MESH
F32, BF16 = jnp.float32, jnp.bfloat16


def gelu_slope(value):
    cdf = 0.5 * (1.0 + lax.erf(value * (1.0 / math.sqrt(2.0))))
    pdf = jnp.exp(-0.5 * value * value) / math.sqrt(2.0 * math.pi)
    return cdf + value * pdf


def encode(term):
    rows, cols = term.shape
    blocks = term.reshape(rows, cols // QBLOCK, QBLOCK)
    scale = (jnp.max(jnp.abs(blocks), axis=2) + 1e-06) / 127.0
    codes = jnp.clip(blocks / scale[:, :, None], -127.0, 127.0).astype(BF16)
    return (codes.reshape(rows, cols), scale)


def decode(codes, scale):
    rows, cols = codes.shape
    blocks = codes.astype(F32).reshape(rows, cols // QBLOCK, QBLOCK)
    return (blocks * scale[:, :, None]).reshape(rows, cols)


def adam(grad, master, moment_one, moment_two):
    new_one = 0.9 * moment_one + 0.1 * grad
    new_two = 0.999 * moment_two + 0.001 * grad * grad
    corr_one = 1.0 - 0.9**ADAM_STEP
    corr_two = 1.0 - 0.999**ADAM_STEP
    update = new_one / corr_one / (jnp.sqrt(new_two / corr_two) + 1e-08) + 0.01 * master
    return master - 0.01 * update, new_one, new_two


def kernel(
    in_hbm, pre_ref, hid_ref, master_ref, one_ref, two_ref,
    gi_ref, nm_ref, n1_ref, n2_ref, nw_ref,
    xin, w_buf, wx, act, act_t, term, xr, zua, zda, sua, sda, zub, zdb, sub, sdb, fxs, fxr, grad_t,
    in_sem, act_s, act_r, ws, wr, wag, nag, rxs, rxr, ras, rar, rbs, rbr, fs, fr,
):
    r = lax.axis_index("dp")
    k = lax.axis_index("tensor")
    z, x = r // X, r % X
    o = 1 - x
    across, above, below = {"dp": r + 1 - 2 * x}, {"dp": r + X}, {"dp": r - X}
    up_ok, dn_ok = z <= Z - 2, z >= 1
    tok, hid = pre_ref.shape
    rows = master_ref.shape[0]
    pend = []

    def when(cond, fn):
        if cond is None:
            fn()
        else:
            pl.when(cond)(fn)

    def rc(src, dst, ssem, rsem, dev):
        return pltpu.make_async_remote_copy(
            src_ref=src, dst_ref=dst, send_sem=ssem, recv_sem=rsem, device_id=dev, device_id_type=MESH
        )

    def send(cond, make):
        when(cond, lambda: make().start())
        pend.append((cond, make))

    def got(cond, make):
        when(cond, lambda: make().wait_recv())

    class Gather:
        def __init__(self, buf, sems, split, on_block):
            self.buf, self.s, self.split, self.on = buf, sems, split, on_block

        def a(self, zz, xx):
            return self.buf.at[X * zz + xx, pl.ds(0, self.split), :]

        def b(self, zz):
            return self.buf.at[pl.ds(X * zz, X), pl.ds(self.split, rows - self.split), :]

        def b1(self, zz, xx):
            return self.buf.at[X * zz + xx, pl.ds(self.split, rows - self.split), :]

        def mk(self, ref, idx, dev):
            return lambda: rc(ref(), ref(), self.s.at[0, idx], self.s.at[1, idx], dev)

        def za(self, s):
            zz_u, zz_d = z - s, z + s
            send(up_ok & (zz_u >= 0), self.mk(lambda: self.a(zz_u, x), s, above))
            send(dn_ok & (zz_d <= Z - 1), self.mk(lambda: self.a(zz_d, x), 3 + s, below))

        def zb(self, s):
            zz_u, zz_d = z - s, z + s
            send(up_ok & (zz_u >= 0), self.mk(lambda: self.b(zz_u), 6 + s, above))
            send(dn_ok & (zz_d <= Z - 1), self.mk(lambda: self.b(zz_d), 9 + s, below))

        def xa(self, cond, zz):
            send(cond, self.mk(lambda: self.a(zz, x), 12 + zz, across))

        def start(self):
            self.xa(None, z)
            self.za(0)
            send(None, self.mk(lambda: self.b1(z, x), 16, across))
            self.on(None, z, x, 0)

        def part_a(self, s):
            zu, zd = z - 1 - s, z + 1 + s
            cu, cd = zu >= 0, zd <= Z - 1
            got(cu, self.mk(lambda: self.a(zu, x), s, above))
            got(cd, self.mk(lambda: self.a(zd, x), 3 + s, below))
            if s + 1 < Z - 1:
                self.za(s + 1)
            self.xa(cu, zu)
            self.xa(cd, zd)
            self.on(cu, zu, x, 0)
            self.on(cd, zd, x, 0)

        def part_b(self, s):
            if s == 0:
                got(None, self.mk(lambda: self.b1(z, o), 16, across))
            else:
                zu, zd = z - s, z + s
                cu, cd = zu >= 0, zd <= Z - 1
                got(cu, self.mk(lambda: self.b(zu), 6 + s - 1, above))
                got(cd, self.mk(lambda: self.b(zd), 9 + s - 1, below))
            if s < Z - 1:
                self.zb(s)
            if s == 0:
                for xx in range(X):
                    self.on(None, z, xx, 1)
            else:
                for xx in range(X):
                    self.on(cu, zu, xx, 1)
                    self.on(cd, zd, xx, 1)

        def finish_x(self):
            for j in range(Z):
                zz = (z + j) % Z
                got(None, self.mk(lambda: self.a(zz, o), 12 + zz, across))
                self.on(None, zz, o, 0)

    def w_part(ref, idx, xx, part):
        lo, n = (0, W_SPLIT) if part == 0 else (W_SPLIT, rows - W_SPLIT)
        return ref.at[idx, xx, pl.ds(lo, n), :]

    def to_tensor(cond, zz, xx, part):
        lo, n = (0, W_SPLIT) if part == 0 else (W_SPLIT, rows - W_SPLIT)
        sem = (zz * X + xx) * 2 + part
        rsem = (k * X + xx) * 2 + part
        c = zz != k
        send(
            c if cond is None else cond & c,
            lambda: rc(
                w_buf.at[X * zz + xx, pl.ds(lo, n), :], w_part(wx, k, xx, part),
                ws.at[sem], wr.at[rsem], {"tensor": zz},
            ),
        )

    gw = Gather(w_buf, wag, W_SPLIT, to_tensor)
    gn = Gather(nw_ref, nag, N_SPLIT, lambda *_: None)

    hi = z // 2
    order = [3 - 3 * hi, 2 - hi, 1 - z + 4 * hi, z]

    def fetch(j):
        blk = X * order[j // 2] + (o if j % 2 == 0 else x)
        col = pl.multiple_of(blk * rows, 128)
        return pltpu.make_async_copy(in_hbm.at[:, pl.ds(col, rows)], xin.at[j], in_sem.at[j])

    for j in range(Z * X):
        fetch(j).start()
    w_buf[r] = master_ref[...].astype(BF16)

    barrier = pltpu.get_barrier_semaphore()

    def hello(dev):
        pl.semaphore_signal(barrier, inc=1, device_id=dev, device_id_type=MESH)

    hello(across)
    when(up_ok, lambda: hello(above))
    when(dn_ok, lambda: hello(below))
    for j in range(1, T):
        hello({"tensor": (k + j) % T})
    pl.semaphore_wait(barrier, T + 1 + z * (Z - 1 - z) // 2)

    gw.start()

    step_t = 256

    @pl.loop(0, tok // step_t)
    def _(i):
        here = pl.ds(pl.multiple_of(i * step_t, step_t), step_t)
        val = hid_ref[here, :].astype(F32) * gelu_slope(pre_ref[here, :].astype(F32))
        act[k, here, :] = val.astype(BF16)
        act_t[:, here] = val.T.astype(BF16)

    def make_term(j):
        blk = X * order[j // 2] + (o if j % 2 == 0 else x)
        fetch(j).wait()

        @pl.loop(0, rows // 256)
        def _(c):
            cols = pl.ds(pl.multiple_of(c * 256, 256), 256)
            t = jnp.dot(act_t[...], xin[j, :, cols], preferred_element_type=F32)
            scale = (jnp.max(jnp.abs(t), axis=0, keepdims=True) + 1e-06) / 127.0
            codes = jnp.clip(t / scale, -127.0, 127.0).astype(BF16)
            term[blk, :, cols] = (codes.astype(F32) * scale).astype(BF16)

    def xr_copy(t, own):
        return lambda: rc(
            term.at[X * t + own, pl.ds(0, G_SPLIT), :], xr.at[t], rxs.at[t], rxr.at[t], across
        )

    for i in range(Z):
        make_term(2 * i)
        send(None, xr_copy(order[i], o))
        make_term(2 * i + 1)
        if i == 0:
            for j in range(1, T):
                kk = (k + j) % T
                send(
                    None,
                    lambda kk=kk, j=j: rc(
                        act.at[k], act.at[k], act_s.at[j - 1], act_r.at[j - 1], {"tensor": kk}
                    ),
                )

    def z_sum(s, value, arrived, zu, zd, su, sd, ssem, rsem):
        tu, td = z + 3 - s, z - 3 + s
        cu, cd = up_ok & (z <= s), dn_ok & (z >= 3 - s)
        for cond, edge, t, zin, out, base, dev in (
            (cu, z == 0, tu, zu, su, 0, above),
            (cd, z == Z - 1, td, zd, sd, 3, below),
        ):
            make = lambda zin=zin, out=out, base=base, dev=dev: rc(
                out.at[s], zin.at[s], ssem.at[base + s], rsem.at[base + s], dev
            )
            def body(edge=edge, t=t, zin=zin, out=out, base=base, dev=dev, make=make):
                arrived(t)
                own = value(t)

                @pl.when(edge)
                def _():
                    out[s] = own().astype(BF16)

                if s > 0:
                    @pl.when(jnp.logical_not(edge))
                    def _():
                        rc(out.at[s], zin.at[s - 1], ssem.at[base + s - 1], rsem.at[base + s - 1], dev).wait_recv()
                        out[s] = (own() + zin[s - 1].astype(F32)).astype(BF16)

            pl.when(cond)(body)
            send(cond, make)

    def value_a(t):
        return lambda: term[X * t + x, :G_SPLIT, :].astype(F32) + xr[t].astype(F32)

    def value_b(t):
        return lambda: term[pl.ds(X * t, X), G_SPLIT:, :].astype(F32)

    def arrived_a(t):
        xr_copy(t, o)().wait_recv()

    def sum_a(s):
        z_sum(s, value_a, arrived_a, zua, zda, sua, sda, ras, rar)

    def sum_b(s):
        z_sum(s, value_b, lambda t: None, zub, zdb, sub, sdb, rbs, rbr)

    sum_b(0)
    gw.part_b(0)
    for s in range(Z - 1):
        sum_a(s)
        gw.part_a(s)
        if s + 1 < Z - 1:
            sum_b(s + 1)
        gw.part_b(s + 1)

    last = Z - 2
    sb = fxs
    sb[...] = term[pl.ds(X * z, X), G_SPLIT:, :].astype(F32)
    for cond, zin, base, dev in ((dn_ok, zub, 0, above), (up_ok, zdb, 3, below)):
        def body(zin=zin, base=base, dev=dev):
            rc(zin.at[last], zin.at[last], rbs.at[base + last], rbr.at[base + last], dev).wait_recv()
            sb[...] += zin[last].astype(F32)
        pl.when(cond)(body)
    fxr[0] = sb[o].astype(BF16)
    fx = lambda: rc(fxr.at[0], fxr.at[1], fs, fr, across)
    send(None, fx)
    arrived_a(z)
    grad_t[:G_SPLIT, :] = value_a(z)()
    for cond, zin, base, dev in ((dn_ok, zua, 0, above), (up_ok, zda, 3, below)):
        def body(zin=zin, base=base, dev=dev):
            rc(zin.at[last], zin.at[last], ras.at[base + last], rar.at[base + last], dev).wait_recv()
            grad_t[:G_SPLIT, :] += zin[last].astype(F32)
        pl.when(cond)(body)
    fx().wait_recv()
    grad_t[G_SPLIT:, :] = sb[x] + fxr[1].astype(F32)

    @pl.loop(0, rows // 256)
    def _(c):
        here = pl.ds(pl.multiple_of(c * 256, 256), 256)
        nm, n1, n2 = adam(
            grad_t[:, here].T, master_ref[here, :], one_ref[here, :], two_ref[here, :]
        )
        nm_ref[here, :] = nm
        n1_ref[here, :] = n1
        n2_ref[here, :] = n2
        nw_ref[r, here, :] = nm.astype(BF16)

    gn.start()
    gw.finish_x()
    for s in range(Z - 1):
        gn.part_b(s)
        gn.part_a(s)
    gn.part_b(Z - 1)

    wx[k] = w_buf[pl.ds(X * k, X)]
    for j in range(1, T):
        src = (k + T - j) % T
        got(None, lambda: rc(act.at[src], act.at[src], act_s.at[j - 1], act_r.at[j - 1], {"tensor": src}))
        for xx in range(X):
            for part in range(2):
                got(
                    None,
                    lambda: rc(
                        w_part(wx, src, xx, part), w_part(wx, src, xx, part),
                        ws.at[0], wr.at[(src * X + xx) * 2 + part], {"tensor": src},
                    ),
                )

    @pl.loop(0, tok // step_t)
    def _(i):
        here = pl.ds(pl.multiple_of(i * step_t, step_t), step_t)
        for xx in range(X):
            total = None
            for src in range(T):
                part = lax.dot_general(
                    act[src, here, :], wx[src, xx], (((1,), (1,)), ((), ())), preferred_element_type=F32
                )
                total = part if total is None else total + part
            gi_ref[here, xx * rows:(xx + 1) * rows] = total.astype(BF16)

    gn.finish_x()
    for cond, make in pend:
        when(cond, lambda: make().wait_send())


def local_kernel(inputs, pre_act, grad_hidden, master, moment_one, moment_two):
    tok, hid = pre_act.shape
    rows = master.shape[0]
    n = Z * X
    gb = hid - G_SPLIT
    vmem = pl.BlockSpec(memory_space=pltpu.VMEM)
    dma = pltpu.SemaphoreType.DMA
    out = pl.pallas_call(
        kernel,
        out_shape=(
            jax.ShapeDtypeStruct((tok, rows * X), BF16),
            jax.ShapeDtypeStruct((rows, hid), F32),
            jax.ShapeDtypeStruct((rows, hid), F32),
            jax.ShapeDtypeStruct((rows, hid), F32),
            jax.ShapeDtypeStruct((n, rows, hid), BF16),
        ),
        in_specs=[pl.BlockSpec(memory_space=pl.ANY)] + [vmem] * 5,
        out_specs=[vmem] * 5,
        scratch_shapes=[
            pltpu.VMEM((n, tok, rows), BF16),
            pltpu.VMEM((n, rows, hid), BF16),
            pltpu.VMEM((T, X, rows, hid), BF16),
            pltpu.VMEM((T, tok, hid), BF16),
            pltpu.VMEM((hid, tok), BF16),
            pltpu.VMEM((n, hid, rows), BF16),
            pltpu.VMEM((Z, G_SPLIT, rows), BF16),
            *[pltpu.VMEM((Z - 1, G_SPLIT, rows), BF16)] * 4,
            *[pltpu.VMEM((Z - 1, X, gb, rows), BF16)] * 4,
            pltpu.VMEM((X, gb, rows), F32),
            pltpu.VMEM((2, gb, rows), BF16),
            pltpu.VMEM((hid, rows), F32),
            dma((n,)), dma((T - 1,)), dma((T - 1,)),
            dma((Z * X * 2,)), dma((T * X * 2,)),
            dma((2, 17)), dma((2, 17)),
            dma((Z,)), dma((Z,)),
            dma((6,)), dma((6,)), dma((6,)), dma((6,)),
            dma(()), dma(()),
        ],
        compiler_params=pltpu.CompilerParams(
            collective_id=0, has_side_effects=True, vmem_limit_bytes=60 * 1024 * 1024
        ),
        cost_estimate=pl.CostEstimate(
            flops=4 * tok * rows * n * hid, bytes_accessed=2 * tok * rows * n * 2, transcendentals=tok * hid
        ),
    )(inputs, pre_act, grad_hidden, master, moment_one, moment_two)
    return (*out[:4], out[4].reshape(n * rows, hid))


def local_plain(inputs, pre_act, grad_hidden, master, moment_one, moment_two):
    act_grad = (grad_hidden.astype(F32) * gelu_slope(pre_act.astype(F32))).astype(BF16)
    weights = lax.all_gather(master.astype(BF16), "dp", axis=0, tiled=True)
    rows = lax.all_to_all(weights, "tensor", split_axis=0, concat_axis=1, tiled=True)
    acts = lax.all_gather(act_grad, "tensor", axis=1, tiled=True)
    grad_input = jnp.einsum("th,dh->td", acts, rows, preferred_element_type=F32).astype(BF16)
    term = jnp.einsum("tr,th->rh", inputs, act_grad, preferred_element_type=F32)
    codes, scale = encode(term)
    grad = lax.psum_scatter(decode(codes, scale), "dp", scatter_dimension=0, tiled=True)
    new_master, new_one, new_two = adam(grad, master, moment_one, moment_two)
    new_weights = lax.all_gather(new_master.astype(BF16), "dp", axis=0, tiled=True)
    return (grad_input, new_master, new_one, new_two, new_weights)


def solution(mesh):
    sizes = dict(mesh.shape)
    body = local_kernel if sizes == {"dp": Z * X, "tensor": T} else local_plain
    two = P("dp", "tensor")
    return jax.shard_map(
        body,
        mesh=mesh,
        in_specs=(P("dp", None), two, two, two, two, two),
        out_specs=(two, two, two, two, P(None, "tensor")),
        check_vma=False,
    )
```

time: 371 us -> 110 us (0.30)
  waiting for transfers between devices: 320 us -> 0 us
  Pallas kernels: 0 us -> 101 us
  matrix products: 18 us -> 0 us
  between operations: 13.8 us -> 0.67 us
  other arithmetic: 7.34 us -> 0 us
    reduce_scatter x2 -> x0, waiting for transfers between devices: 212 us -> none  [the longest x1 116 us: local(): lax.psum_scatter(decode(codes, scale), 'dp', scatter_dimension=0, tiled=T...]
    all_gather x2 -> x0, waiting for transfers between devices: 107 us -> none  [the longest x1 59.3 us: local(): lax.all_gather(weights, 'dp', axis=0, tiled=True)]
    pallas_call x0 -> x1, Pallas kernels: none -> 101 us  [local_kernel(): pl.pallas_call(kernel, out_shape=(jax.ShapeDtypeStruct((tok, rows * X), B...]
    dot_general x2 -> x0, matrix products: 18 us -> none  [the longest x1 10.5 us: local(): jnp.einsum('th,dh->td', act_grad, lax.all_gather(weights, 'dp', axis=0, t...]
    convert_element_type x2 -> x0, other arithmetic: 3.76 us -> none  [the longest x1 2.97 us: local(): new_master.astype(jnp.bfloat16)]
  transfers between devices with their start and end apart: 4 -> 0, of which waited for: 4 -> 0; matrix products, arithmetic and copies ran while one was open for 7% -> 0% of each run, Pallas kernels for 0% -> 0%
where the time goes in v1:
time: 110 us
  Pallas kernels  101 us (92%)
  local copies, waits for them, and re-layouts  8.23 us (7%)
    pallas_call x1, Pallas kernels, local_kernel(): pl.pallas_call(kernel, out_shape=(jax.ShapeDtypeStruct((tok, rows * X), B...  101 us
    unnamed x13, local copies, waits for them, and re-layouts  8.23 us

profile of v1, /device:TPU:0, one launch (start us, length us, event | category | flops | bytes accessed | tf_op | source)
XLA Modules:
  0.0 110.3 jit_solution(1595706938548072840)
XLA Ops:
  0.6 101.4 %shard_map.101 = (bf16[1024,1536]{1,0:T(8,128)(2,1)}, f32[768,256]{1,0:T(8,128)}, f32[768,256]{1,0:T(8,128)}, f32[768,256]{1,0:T(8,128)}, bf16[8,768,256]{2,1,0:T(8,128)(2,1)}) custom-call(bf16[1024,6144]{1,0:T(8,128)(2,1)} %in_hbm.1, bf16[1024,256]{1,0:T(8,128)(2,1)} %pre_ref.1, bf16[1024,256]{1,0:T(8,128)(2,1)} %hid_ref.1, f32[768,256]{1,0:T(8,128)} %master_ref.1, ...), custom_call_target="tpu_custom_call" | custom-call | flops 6442450944 | bytes 25165824 | tf_op jit(solution)/shard_map/pallas_call | solution.py:369
  102.0 0.0 copy-start.3
  102.1 0.0 copy-start.2
  102.1 0.0 copy-start.1
  102.1 3.9 %copy.16 = bf16[1024,1536]{1,0:T(8,128)(2,1)} copy(bf16[1024,1536]{1,0:T(8,128)(2,1)} %get-tuple-element.20) | data formatting | bytes 6291456
  106.0 0.0 copy-done.3
  106.0 0.0 copy-start
  106.0 0.9 copy.17
  106.9 0.0 copy-done.2
  106.9 0.9 copy.18
  107.7 0.0 copy-done.1
  107.8 0.9 copy.19
  108.6 0.0 copy-done
  108.6 1.7 %copy.20 = bf16[6144,256]{1,0:T(8,128)(2,1)} copy(bf16[6144,256]{1,0:T(8,128)(2,1)S(1)} %bitcast.1) | data formatting | bytes 6291456
Async XLA Ops:
  102.0 3.9 %copy-start.3 = (f32[768,256]{1,0:T(8,128)S(1)}, f32[768,256]{1,0:T(8,128)}, u32[]{:S(2)}) copy-start(f32[768,256]{1,0:T(8,128)} %get-tuple-element.21) | copy-start | bytes 2359300
  102.1 4.8 %copy-start.2 = (f32[768,256]{1,0:T(8,128)S(1)}, f32[768,256]{1,0:T(8,128)}, u32[]{:S(2)}) copy-start(f32[768,256]{1,0:T(8,128)} %get-tuple-element.22) | copy-start | bytes 2359300
  102.1 5.7 %copy-start.1 = (f32[768,256]{1,0:T(8,128)S(1)}, f32[768,256]{1,0:T(8,128)}, u32[]{:S(2)}) copy-start(f32[768,256]{1,0:T(8,128)} %get-tuple-element.23) | copy-start | bytes 2359300
  106.0 2.6 %copy-start = (bf16[8,768,256]{2,1,0:T(8,128)(2,1)S(1)}, bf16[8,768,256]{2,1,0:T(8,128)(2,1)}, u32[]{:S(2)}) copy-start(bf16[8,768,256]{2,1,0:T(8,128)(2,1)} %get-tuple-element.14) | copy-start | bytes 9437188

commit v2 on v1

--- a/solution.py
+++ b/solution.py
@@ -11,9 +11,9 @@
 QBLOCK = 256
 ADAM_STEP = 10
 Z, X, T = 4, 2, 4
-W_SPLIT = 464
+W_SPLIT = 544
 G_SPLIT = 160
-N_SPLIT = 640
+N_SPLIT = 576
 MESH = pl.DeviceIdType.MESH
 F32, BF16 = jnp.float32, jnp.bfloat16
 
@@ -48,10 +48,11 @@
 
 
 def kernel(
-    in_hbm, pre_ref, hid_ref, master_ref, one_ref, two_ref,
-    gi_ref, nm_ref, n1_ref, n2_ref, nw_ref,
+    in_hbm, pre_ref, hid_ref, master_ref, one_hbm, two_hbm,
+    gi_hbm, grad_hbm, nw_hbm,
+    gi_ref, grad_ref, nw_ref, one_ref, two_ref,
     xin, w_buf, wx, act, act_t, term, xr, zua, zda, sua, sda, zub, zdb, sub, sdb, fxs, fxr, grad_t,
-    in_sem, act_s, act_r, ws, wr, wag, nag, rxs, rxr, ras, rar, rbs, rbr, fs, fr,
+    out_sem, mom_sem, in_sem, act_s, act_r, ws, wr, wag, nag, rxs, rxr, ras, rar, rbs, rbr, fs, fr,
 ):
     r = lax.axis_index("dp")
     k = lax.axis_index("tensor")
@@ -146,8 +147,8 @@
                     self.on(cu, zu, xx, 1)
                     self.on(cd, zd, xx, 1)
 
-        def finish_x(self):
-            for j in range(Z):
+        def finish_x(self, *only):
+            for j in only or range(Z):
                 zz = (z + j) % Z
                 got(None, self.mk(lambda: self.a(zz, o), 12 + zz, across))
                 self.on(None, zz, o, 0)
@@ -182,6 +183,12 @@
 
     for j in range(Z * X):
         fetch(j).start()
+    moments = [
+        pltpu.make_async_copy(one_hbm, one_ref, mom_sem.at[0]),
+        pltpu.make_async_copy(two_hbm, two_ref, mom_sem.at[1]),
+    ]
+    for c in moments:
+        c.start()
     w_buf[r] = master_ref[...].astype(BF16)
 
     barrier = pltpu.get_barrier_semaphore()
@@ -282,12 +289,13 @@
 
     sum_b(0)
     gw.part_b(0)
-    for s in range(Z - 1):
-        sum_a(s)
-        gw.part_a(s)
-        if s + 1 < Z - 1:
-            sum_b(s + 1)
-        gw.part_b(s + 1)
+    sum_a(0)
+    gw.part_a(0)
+    sum_b(1)
+    sum_a(1)
+    sum_b(2)
+    sum_a(2)
+    gw.part_b(1)
 
     last = Z - 2
     sb = fxs
@@ -300,6 +308,7 @@
     fxr[0] = sb[o].astype(BF16)
     fx = lambda: rc(fxr.at[0], fxr.at[1], fs, fr, across)
     send(None, fx)
+    gw.part_a(1)
     arrived_a(z)
     grad_t[:G_SPLIT, :] = value_a(z)()
     for cond, zin, base, dev in ((dn_ok, zua, 0, above), (up_ok, zda, 3, below)):
@@ -310,23 +319,31 @@
     fx().wait_recv()
     grad_t[G_SPLIT:, :] = sb[x] + fxr[1].astype(F32)
 
+    for c in moments:
+        c.wait()
+
     @pl.loop(0, rows // 256)
     def _(c):
         here = pl.ds(pl.multiple_of(c * 256, 256), 256)
-        nm, n1, n2 = adam(
-            grad_t[:, here].T, master_ref[here, :], one_ref[here, :], two_ref[here, :]
-        )
-        nm_ref[here, :] = nm
-        n1_ref[here, :] = n1
-        n2_ref[here, :] = n2
-        nw_ref[r, here, :] = nm.astype(BF16)
+        grad = grad_t[:, here].T
+        grad_ref[here, :] = grad
+        new_master = adam(grad, master_ref[here, :], one_ref[here, :], two_ref[here, :])[0]
+        nw_ref[r, here, :] = new_master.astype(BF16)
 
     gn.start()
+    grad_out = pltpu.make_async_copy(grad_ref, grad_hbm, mom_sem.at[0])
+    grad_out.start()
+    gw.part_b(2)
+    gw.part_a(2)
+    gn.part_b(0)
+    gn.part_a(0)
+    gw.part_b(3)
+    gn.part_b(1)
+    gn.part_a(1)
     gw.finish_x()
-    for s in range(Z - 1):
-        gn.part_b(s)
-        gn.part_a(s)
-    gn.part_b(Z - 1)
+    gn.part_b(2)
+    gn.part_a(2)
+    gn.part_b(3)
 
     wx[k] = w_buf[pl.ds(X * k, X)]
     for j in range(1, T):
@@ -342,9 +359,15 @@
                     ),
                 )
 
-    @pl.loop(0, tok // step_t)
-    def _(i):
-        here = pl.ds(pl.multiple_of(i * step_t, step_t), step_t)
+    writes = []
+
+    def write(src, dst):
+        c = pltpu.make_async_copy(src, dst, out_sem.at[len(writes)])
+        c.start()
+        writes.append(c)
+
+    for i in range(tok // step_t):
+        here = pl.ds(i * step_t, step_t)
         for xx in range(X):
             total = None
             for src in range(T):
@@ -353,8 +376,15 @@
                 )
                 total = part if total is None else total + part
             gi_ref[here, xx * rows:(xx + 1) * rows] = total.astype(BF16)
-
-    gn.finish_x()
+        write(gi_ref.at[here, :], gi_hbm.at[here, :])
+
+    for j in range(Z):
+        gn.finish_x(j)
+        both = pl.ds(X * ((z + j) % Z), X)
+        write(nw_ref.at[both], nw_hbm.at[both])
+    for c in writes:
+        c.wait()
+    grad_out.wait()
     for cond, make in pend:
         when(cond, lambda: make().wait_send())
 
@@ -366,18 +396,22 @@
     gb = hid - G_SPLIT
     vmem = pl.BlockSpec(memory_space=pltpu.VMEM)
     dma = pltpu.SemaphoreType.DMA
-    out = pl.pallas_call(
+    anywhere = pl.BlockSpec(memory_space=pl.ANY)
+    grad_input, grad, new_weights = pl.pallas_call(
         kernel,
         out_shape=(
             jax.ShapeDtypeStruct((tok, rows * X), BF16),
             jax.ShapeDtypeStruct((rows, hid), F32),
-            jax.ShapeDtypeStruct((rows, hid), F32),
-            jax.ShapeDtypeStruct((rows, hid), F32),
             jax.ShapeDtypeStruct((n, rows, hid), BF16),
         ),
-        in_specs=[pl.BlockSpec(memory_space=pl.ANY)] + [vmem] * 5,
-        out_specs=[vmem] * 5,
+        in_specs=[anywhere, vmem, vmem, vmem, anywhere, anywhere],
+        out_specs=[anywhere] * 3,
         scratch_shapes=[
+            pltpu.VMEM((tok, rows * X), BF16),
+            pltpu.VMEM((rows, hid), F32),
+            pltpu.VMEM((n, rows, hid), BF16),
+            pltpu.VMEM((rows, hid), F32),
+            pltpu.VMEM((rows, hid), F32),
             pltpu.VMEM((n, tok, rows), BF16),
             pltpu.VMEM((n, rows, hid), BF16),
             pltpu.VMEM((T, X, rows, hid), BF16),
@@ -390,7 +424,7 @@
             pltpu.VMEM((X, gb, rows), F32),
             pltpu.VMEM((2, gb, rows), BF16),
             pltpu.VMEM((hid, rows), F32),
-            dma((n,)), dma((T - 1,)), dma((T - 1,)),
+            dma((tok // 256 + Z,)), dma((2,)), dma((n,)), dma((T - 1,)), dma((T - 1,)),
             dma((Z * X * 2,)), dma((T * X * 2,)),
             dma((2, 17)), dma((2, 17)),
             dma((Z,)), dma((Z,)),
@@ -404,7 +438,8 @@
             flops=4 * tok * rows * n * hid, bytes_accessed=2 * tok * rows * n * 2, transcendentals=tok * hid
         ),
     )(inputs, pre_act, grad_hidden, master, moment_one, moment_two)
-    return (*out[:4], out[4].reshape(n * rows, hid))
+    new_master, new_one, new_two = adam(grad, master, moment_one, moment_two)
+    return (grad_input, new_master, new_one, new_two, new_weights.reshape(n * rows, hid))
 
 
 def local_plain(inputs, pre_act, grad_hidden, master, moment_one, moment_two):

time: 110 us -> 116 us (1.055)
  Pallas kernels: 101 us -> 107 us
  local copies, waits for them, and re-layouts: 8.23 us -> 4.71 us
  other arithmetic: 0 us -> 3.05 us
    pallas_call x1, Pallas kernels: 101 us -> 107 us  [local_kernel(): pl.pallas_call(kernel, out_shape=(jax.ShapeDtypeStruct((tok, rows * X), B...]
    unnamed x13 -> x12, local copies, waits for them, and re-layouts: 8.23 us -> 4.71 us
    sub x0 -> x1, other arithmetic: none -> 3.05 us  [adam(): return (master - 0.01 * update, new_one, new_two)]
where the time goes in v2:
time: 116 us; the launch traced here: 115 us
  Pallas kernels  107 us (92%)
  local copies, waits for them, and re-layouts  4.71 us (4%)
  other arithmetic  3.05 us (3%)
    pallas_call x1, Pallas kernels, local_kernel(): pl.pallas_call(kernel, out_shape=(jax.ShapeDtypeStruct((tok, rows * X), B...  107 us
    unnamed x12, local copies, waits for them, and re-layouts  4.71 us
    sub x1, other arithmetic, adam(): return (master - 0.01 * update, new_one, new_two)  3.05 us

profile of v2, /device:TPU:0, one launch (start us, length us, event | category | flops | bytes accessed | tf_op | source)
XLA Modules:
  0.0 115.4 jit_solution(12596960346186034371)
XLA Ops:
  0.6 0.0 copy-start.4
  0.6 0.0 copy-start.3
  0.7 0.0 copy-start.2
  0.7 107.0 %shard_map.101 = (bf16[1024,1536]{1,0:T(8,128)(2,1)}, f32[768,256]{1,0:T(8,128)}, bf16[8,768,256]{2,1,0:T(8,128)(2,1)}) custom-call(bf16[1024,6144]{1,0:T(8,128)(2,1)} %in_hbm.1, bf16[1024,256]{1,0:T(8,128)(2,1)} %pre_ref.1, bf16[1024,256]{1,0:T(8,128)(2,1)} %hid_ref.1, f32[768,256]{1,0:T(8,128)} %master_ref.1, f32[768,256]{1,0:T(8,128)} %one_hbm.1, ...), custom_call_target="tpu_custom_call" | custom-call | flops 6442450944 | bytes 25165824 | tf_op jit(solution)/shard_map/pallas_call | solution.py:400
  107.6 0.0 copy-start.1
  107.6 0.0 copy-done.4
  107.6 0.0 copy-done.3
  107.7 0.0 copy-done.2
  107.7 3.0 %multiply_subtract_fusion = (f32[768,256]{1,0:T(8,128)}, f32[768,256]{1,0:T(8,128)}, f32[768,256]{1,0:T(8,128)}) fusion(f32[768,256]{1,0:T(8,128)S(1)} %copy-done.2, f32[768,256]{1,0:T(8,128)} %get-tuple-element.9, f32[768,256]{1,0:T(8,128)S(1)} %copy-done.3, f32[768,256]{1,0:T(8,128)S(1)} %copy-done.4), kind=kLoop, calls=%fused_computation.2 | loop fusion | flops 2949120 | bytes 5505024 | tf_op jit(solution)/shard_map/sub | solution.py:47
  110.7 0.0 copy-done.1
  110.7 0.0 copy-start
  110.7 1.7 %copy.13 = bf16[1024,1536]{1,0:T(8,128)(2,1)} copy(bf16[1024,1536]{1,0:T(8,128)(2,1)S(1)} %copy-done.1) | data formatting | bytes 6291456
  112.4 1.4 %copy-done = bf16[8,768,256]{2,1,0:T(8,128)(2,1)S(1)} copy-done((bf16[8,768,256]{2,1,0:T(8,128)(2,1)S(1)}, bf16[8,768,256]{2,1,0:T(8,128)(2,1)}, u32[]{:S(2)}) %copy-start) | copy-done | bytes 3145752
  113.7 1.7 %copy.14 = bf16[6144,256]{1,0:T(8,128)(2,1)} copy(bf16[6144,256]{1,0:T(8,128)(2,1)S(1)} %bitcast.1) | data formatting | bytes 6291456
Async XLA Ops:
  0.6 107.0 %copy-start.4 = (f32[768,256]{1,0:T(8,128)S(1)}, f32[768,256]{1,0:T(8,128)}, u32[]{:S(2)}) copy-start(f32[768,256]{1,0:T(8,128)} %two_hbm.1) | copy-start | bytes 2359300
  0.6 107.0 %copy-start.3 = (f32[768,256]{1,0:T(8,128)S(1)}, f32[768,256]{1,0:T(8,128)}, u32[]{:S(2)}) copy-start(f32[768,256]{1,0:T(8,128)} %one_hbm.1) | copy-start | bytes 2359300
  0.7 107.0 %copy-start.2 = (f32[768,256]{1,0:T(8,128)S(1)}, f32[768,256]{1,0:T(8,128)}, u32[]{:S(2)}) copy-start(f32[768,256]{1,0:T(8,128)} %master_ref.1) | copy-start | bytes 2359300
  107.6 3.1 %copy-start.1 = (bf16[1024,1536]{1,0:T(8,128)(2,1)S(1)}, bf16[1024,1536]{1,0:T(8,128)(2,1)}, u32[]{:S(2)}) copy-start(bf16[1024,1536]{1,0:T(8,128)(2,1)} %get-tuple-element.19) | copy-start | bytes 9437188
  110.7 3.0 %copy-start = (bf16[8,768,256]{2,1,0:T(8,128)(2,1)S(1)}, bf16[8,768,256]{2,1,0:T(8,128)(2,1)}, u32[]{:S(2)}) copy-start(bf16[8,768,256]{2,1,0:T(8,128)(2,1)} %get-tuple-element.10) | copy-start | bytes 9437188

commit v3 on v1

--- a/solution.py
+++ b/solution.py
@@ -13,7 +13,8 @@
 Z, X, T = 4, 2, 4
 W_SPLIT = 464
 G_SPLIT = 160
-N_SPLIT = 640
+N_SPLIT = 320
+PIECES = 4
 MESH = pl.DeviceIdType.MESH
 F32, BF16 = jnp.float32, jnp.bfloat16
 
@@ -48,10 +49,11 @@
 
 
 def kernel(
-    in_hbm, pre_ref, hid_ref, master_ref, one_ref, two_ref,
-    gi_ref, nm_ref, n1_ref, n2_ref, nw_ref,
+    in_hbm, pre_ref, hid_ref, master_ref, one_hbm, two_hbm,
+    gi_hbm, nm_hbm, n1_hbm, n2_hbm, nw_hbm,
+    gi_ref, nm_ref, n1_ref, n2_ref, nw_ref, one_ref, two_ref,
     xin, w_buf, wx, act, act_t, term, xr, zua, zda, sua, sda, zub, zdb, sub, sdb, fxs, fxr, grad_t,
-    in_sem, act_s, act_r, ws, wr, wag, nag, rxs, rxr, ras, rar, rbs, rbr, fs, fr,
+    out_sem, mom_sem, in_sem, act_s, act_r, ws, wr, wag, nag, mag, rxs, rxr, ras, rar, rbs, rbr, fs, fr,
 ):
     r = lax.axis_index("dp")
     k = lax.axis_index("tensor")
@@ -82,17 +84,19 @@
         when(cond, lambda: make().wait_recv())
 
     class Gather:
-        def __init__(self, buf, sems, split, on_block):
-            self.buf, self.s, self.split, self.on = buf, sems, split, on_block
+        def __init__(self, buf, sems, first, split, end, on_block, late):
+            self.buf, self.s, self.on = buf, sems, on_block
+            self.rows_a, self.rows_b = pl.ds(first, split - first), pl.ds(split, end - split)
+            self.late, self.kept = late, []
 
         def a(self, zz, xx):
-            return self.buf.at[X * zz + xx, pl.ds(0, self.split), :]
+            return self.buf.at[X * zz + xx, self.rows_a, :]
 
         def b(self, zz):
-            return self.buf.at[pl.ds(X * zz, X), pl.ds(self.split, rows - self.split), :]
+            return self.buf.at[pl.ds(X * zz, X), self.rows_b, :]
 
         def b1(self, zz, xx):
-            return self.buf.at[X * zz + xx, pl.ds(self.split, rows - self.split), :]
+            return self.buf.at[X * zz + xx, self.rows_b, :]
 
         def mk(self, ref, idx, dev):
             return lambda: rc(ref(), ref(), self.s.at[0, idx], self.s.at[1, idx], dev)
@@ -108,6 +112,17 @@
             send(dn_ok & (zz_d <= Z - 1), self.mk(lambda: self.b(zz_d), 9 + s, below))
 
         def xa(self, cond, zz):
+            if self.late:
+                self.kept.append((cond, zz))
+            else:
+                self.xa_now(cond, zz)
+
+        def flush(self):
+            for cond, zz in self.kept:
+                self.xa_now(cond, zz)
+            self.kept = []
+
+        def xa_now(self, cond, zz):
             send(cond, self.mk(lambda: self.a(zz, x), 12 + zz, across))
 
         def start(self):
@@ -146,8 +161,8 @@
                     self.on(cu, zu, xx, 1)
                     self.on(cd, zd, xx, 1)
 
-        def finish_x(self):
-            for j in range(Z):
+        def finish_x(self, *only):
+            for j in only or range(Z):
                 zz = (z + j) % Z
                 got(None, self.mk(lambda: self.a(zz, o), 12 + zz, across))
                 self.on(None, zz, o, 0)
@@ -169,8 +184,12 @@
             ),
         )
 
-    gw = Gather(w_buf, wag, W_SPLIT, to_tensor)
-    gn = Gather(nw_ref, nag, N_SPLIT, lambda *_: None)
+    half = rows // 2
+    gw = Gather(w_buf, wag, 0, W_SPLIT, rows, to_tensor, True)
+    gn, gm = [
+        Gather(nw_ref, sems, i * half, i * half + N_SPLIT, (i + 1) * half, lambda *_: None, False)
+        for i, sems in enumerate((nag, mag))
+    ]
 
     hi = z // 2
     order = [3 - 3 * hi, 2 - hi, 1 - z + 4 * hi, z]
@@ -182,6 +201,12 @@
 
     for j in range(Z * X):
         fetch(j).start()
+    moments = [
+        pltpu.make_async_copy(one_hbm, one_ref, mom_sem.at[0]),
+        pltpu.make_async_copy(two_hbm, two_ref, mom_sem.at[1]),
+    ]
+    for c in moments:
+        c.start()
     w_buf[r] = master_ref[...].astype(BF16)
 
     barrier = pltpu.get_barrier_semaphore()
@@ -284,6 +309,8 @@
     gw.part_b(0)
     for s in range(Z - 1):
         sum_a(s)
+        if s == 1:
+            gw.flush()
         gw.part_a(s)
         if s + 1 < Z - 1:
             sum_b(s + 1)
@@ -308,25 +335,45 @@
             grad_t[:G_SPLIT, :] += zin[last].astype(F32)
         pl.when(cond)(body)
     fx().wait_recv()
+    gw.flush()
     grad_t[G_SPLIT:, :] = sb[x] + fxr[1].astype(F32)
 
-    @pl.loop(0, rows // 256)
-    def _(c):
-        here = pl.ds(pl.multiple_of(c * 256, 256), 256)
-        nm, n1, n2 = adam(
-            grad_t[:, here].T, master_ref[here, :], one_ref[here, :], two_ref[here, :]
-        )
-        nm_ref[here, :] = nm
-        n1_ref[here, :] = n1
-        n2_ref[here, :] = n2
-        nw_ref[r, here, :] = nm.astype(BF16)
-
-    gn.start()
-    gw.finish_x()
+    for c in moments:
+        c.wait()
+
+    for g, part in ((gn, 0), (gm, 1)):
+        @pl.loop(0, half // 128)
+        def _(c, part=part):
+            here = pl.ds(pl.multiple_of(part * half + c * 128, 128), 128)
+            nm, n1, n2 = adam(
+                grad_t[:, here].T, master_ref[here, :], one_ref[here, :], two_ref[here, :]
+            )
+            nm_ref[here, :] = nm
+            n1_ref[here, :] = n1
+            n2_ref[here, :] = n2
+            nw_ref[r, here, :] = nm.astype(BF16)
+
+        g.start()
+
+    writes = []
+
+    def write(src, dst):
+        c = pltpu.make_async_copy(src, dst, out_sem.at[len(writes)])
+        c.start()
+        writes.append(c)
+
+    write(nm_ref, nm_hbm)
+    write(n1_ref, n1_hbm)
+    write(n2_ref, n2_hbm)
     for s in range(Z - 1):
+        gn.part_a(s)
+        gm.part_a(s)
         gn.part_b(s)
-        gn.part_a(s)
+        gm.part_b(s)
+        if s == 1:
+            gw.finish_x()
     gn.part_b(Z - 1)
+    gm.part_b(Z - 1)
 
     wx[k] = w_buf[pl.ds(X * k, X)]
     for j in range(1, T):
@@ -342,9 +389,8 @@
                     ),
                 )
 
-    @pl.loop(0, tok // step_t)
-    def _(i):
-        here = pl.ds(pl.multiple_of(i * step_t, step_t), step_t)
+    for i in range(tok // step_t):
+        here = pl.ds(i * step_t, step_t)
         for xx in range(X):
             total = None
             for src in range(T):
@@ -353,10 +399,31 @@
                 )
                 total = part if total is None else total + part
             gi_ref[here, xx * rows:(xx + 1) * rows] = total.astype(BF16)
-
-    gn.finish_x()
+        write(gi_ref.at[here, :], gi_hbm.at[here, :])
+
+    for j in range(Z):
+        gn.finish_x(j)
+        gm.finish_x(j)
+        both = pl.ds(X * ((z + j) % Z), X)
+        write(nw_ref.at[both], nw_hbm.at[both])
+    for c in writes:
+        c.wait()
     for cond, make in pend:
         when(cond, lambda: make().wait_send())
+
+
+def place(*refs):
+    srcs, dsts, sems = refs[:5], refs[5:10], refs[10]
+    copies = []
+    for src, dst in zip(srcs, dsts):
+        step = src.shape[0] // PIECES
+        for i in range(PIECES):
+            here = pl.ds(i * step, step)
+            copies.append(pltpu.make_async_copy(src.at[here], dst.at[here], sems.at[len(copies)]))
+    for c in copies:
+        c.start()
+    for c in copies:
+        c.wait()
 
 
 def local_kernel(inputs, pre_act, grad_hidden, master, moment_one, moment_two):
@@ -366,18 +433,22 @@
     gb = hid - G_SPLIT
     vmem = pl.BlockSpec(memory_space=pltpu.VMEM)
     dma = pltpu.SemaphoreType.DMA
+    anywhere, hbm = pl.BlockSpec(memory_space=pl.ANY), pl.BlockSpec(memory_space=pltpu.HBM)
     out = pl.pallas_call(
         kernel,
         out_shape=(
             jax.ShapeDtypeStruct((tok, rows * X), BF16),
-            jax.ShapeDtypeStruct((rows, hid), F32),
-            jax.ShapeDtypeStruct((rows, hid), F32),
-            jax.ShapeDtypeStruct((rows, hid), F32),
+            *[jax.ShapeDtypeStruct((rows, hid), F32)] * 3,
             jax.ShapeDtypeStruct((n, rows, hid), BF16),
         ),
-        in_specs=[pl.BlockSpec(memory_space=pl.ANY)] + [vmem] * 5,
-        out_specs=[vmem] * 5,
+        in_specs=[anywhere, vmem, vmem, vmem, anywhere, anywhere],
+        out_specs=[anywhere] * 5,
         scratch_shapes=[
+            pltpu.VMEM((tok, rows * X), BF16),
+            *[pltpu.VMEM((rows, hid), F32)] * 3,
+            pltpu.VMEM((n, rows, hid), BF16),
+            pltpu.VMEM((rows, hid), F32),
+            pltpu.VMEM((rows, hid), F32),
             pltpu.VMEM((n, tok, rows), BF16),
             pltpu.VMEM((n, rows, hid), BF16),
             pltpu.VMEM((T, X, rows, hid), BF16),
@@ -390,9 +461,9 @@
             pltpu.VMEM((X, gb, rows), F32),
             pltpu.VMEM((2, gb, rows), BF16),
             pltpu.VMEM((hid, rows), F32),
-            dma((n,)), dma((T - 1,)), dma((T - 1,)),
+            dma((tok // 256 + Z + 3,)), dma((2,)), dma((n,)), dma((T - 1,)), dma((T - 1,)),
             dma((Z * X * 2,)), dma((T * X * 2,)),
-            dma((2, 17)), dma((2, 17)),
+            dma((2, 17)), dma((2, 17)), dma((2, 17)),
             dma((Z,)), dma((Z,)),
             dma((6,)), dma((6,)), dma((6,)), dma((6,)),
             dma(()), dma(()),
@@ -404,6 +475,15 @@
             flops=4 * tok * rows * n * hid, bytes_accessed=2 * tok * rows * n * 2, transcendentals=tok * hid
         ),
     )(inputs, pre_act, grad_hidden, master, moment_one, moment_two)
+    out = pl.pallas_call(
+        place,
+        out_shape=tuple(jax.ShapeDtypeStruct(a.shape, a.dtype) for a in out),
+        in_specs=[hbm] * 5,
+        out_specs=[hbm] * 5,
+        scratch_shapes=[dma((5 * PIECES,))],
+        compiler_params=pltpu.CompilerParams(vmem_limit_bytes=60 * 1024 * 1024),
+        cost_estimate=pl.CostEstimate(flops=0, bytes_accessed=2 * 9 * 2**20, transcendentals=0),
+    )(*out)
     return (*out[:4], out[4].reshape(n * rows, hid))
 
 

time: 110 us -> 369 us (3.35)
  Pallas kernels: 101 us -> 368 us
  local copies, waits for them, and re-layouts: 8.23 us -> 0 us
    pallas_call x0 -> x1, Pallas kernels: none -> 263 us  [local_kernel(): pl.pallas_call(place, out_shape=tuple((jax.ShapeDtypeStruct(a.shape, a.dt...]
    unnamed x13 -> x0, local copies, waits for them, and re-layouts: 8.23 us -> none
where the time goes in v3:
time: 369 us; the launch traced here: 368 us
  Pallas kernels  368 us (100%)
    pallas_call x1, Pallas kernels, local_kernel(): pl.pallas_call(place, out_shape=tuple((jax.ShapeDtypeStruct(a.shape, a.dt...  263 us
    pallas_call x1, Pallas kernels, local_kernel(): pl.pallas_call(kernel, out_shape=(jax.ShapeDtypeStruct((tok, rows * X), B...  104 us

profile of v3, /device:TPU:0, one launch (start us, length us, event | category | flops | bytes accessed | tf_op | source)
XLA Modules:
  0.0 368.4 jit_solution(18359624834528522208)
XLA Ops:
  0.6 104.4 %shard_map.101 = (bf16[1024,1536]{1,0:T(8,128)(2,1)}, f32[768,256]{1,0:T(8,128)}, f32[768,256]{1,0:T(8,128)}, f32[768,256]{1,0:T(8,128)}, bf16[8,768,256]{2,1,0:T(8,128)(2,1)}) custom-call(bf16[1024,6144]{1,0:T(8,128)(2,1)} %in_hbm.1, bf16[1024,256]{1,0:T(8,128)(2,1)} %pre_ref.1, bf16[1024,256]{1,0:T(8,128)(2,1)} %hid_ref.1, f32[768,256]{1,0:T(8,128)} %master_ref.1, ...), custom_call_target="tpu_custom_call" | custom-call | flops 6442450944 | bytes 25165824 | tf_op jit(solution)/shard_map/pallas_call | solution.py:437
  105.1 263.3 %shard_map.102 = (bf16[1024,1536]{1,0:T(8,128)(2,1)}, f32[768,256]{1,0:T(8,128)}, f32[768,256]{1,0:T(8,128)}, f32[768,256]{1,0:T(8,128)}, bf16[8,768,256]{2,1,0:T(8,128)(2,1)}) custom-call(bf16[1024,1536]{1,0:T(8,128)(2,1)} %get-tuple-element.15.refs_0_, f32[768,256]{1,0:T(8,128)} %get-tuple-element.16.refs_1_, f32[768,256]{1,0:T(8,128)} %get-tuple-element.17.refs_2_, ...), custom_call_target="tpu_custom_call" | custom-call | bytes 18874368 | tf_op jit(solution)/shard_map/pallas_call | solution.py:478

commit v4 on v3

--- a/solution.py
+++ b/solution.py
@@ -13,7 +13,7 @@
 Z, X, T = 4, 2, 4
 W_SPLIT = 464
 G_SPLIT = 160
-N_SPLIT = 320
+N_SPLIT = 352
 PIECES = 4
 MESH = pl.DeviceIdType.MESH
 F32, BF16 = jnp.float32, jnp.bfloat16
@@ -185,7 +185,7 @@
         )
 
     half = rows // 2
-    gw = Gather(w_buf, wag, 0, W_SPLIT, rows, to_tensor, True)
+    gw = Gather(w_buf, wag, 0, W_SPLIT, rows, to_tensor, False)
     gn, gm = [
         Gather(nw_ref, sems, i * half, i * half + N_SPLIT, (i + 1) * half, lambda *_: None, False)
         for i, sems in enumerate((nag, mag))
@@ -232,28 +232,31 @@
         act[k, here, :] = val.astype(BF16)
         act_t[:, here] = val.T.astype(BF16)
 
-    def make_term(j):
+    def make_term(h, j):
         blk = X * order[j // 2] + (o if j % 2 == 0 else x)
-        fetch(j).wait()
-
-        @pl.loop(0, rows // 256)
+        if h == 0:
+            fetch(j).wait()
+
+        @pl.loop(0, half // 128)
         def _(c):
-            cols = pl.ds(pl.multiple_of(c * 256, 256), 256)
+            at = pl.multiple_of(c * 128, 128)
+            cols = pl.ds(h * half + at, 128)
             t = jnp.dot(act_t[...], xin[j, :, cols], preferred_element_type=F32)
             scale = (jnp.max(jnp.abs(t), axis=0, keepdims=True) + 1e-06) / 127.0
             codes = jnp.clip(t / scale, -127.0, 127.0).astype(BF16)
-            term[blk, :, cols] = (codes.astype(F32) * scale).astype(BF16)
-
-    def xr_copy(t, own):
+            term[h, blk, :, pl.ds(at, 128)] = (codes.astype(F32) * scale).astype(BF16)
+
+    def xr_copy(h, t, own):
         return lambda: rc(
-            term.at[X * t + own, pl.ds(0, G_SPLIT), :], xr.at[t], rxs.at[t], rxr.at[t], across
+            term.at[h, X * t + own, pl.ds(0, G_SPLIT), :], xr.at[h, t], rxs.at[h, t], rxr.at[h, t], across
         )
 
-    for i in range(Z):
-        make_term(2 * i)
-        send(None, xr_copy(order[i], o))
-        make_term(2 * i + 1)
-        if i == 0:
+    for h in range(2):
+        for i in range(Z):
+            make_term(h, 2 * i)
+            send(None, xr_copy(h, order[i], o))
+            make_term(h, 2 * i + 1)
+        if h == 0:
             for j in range(1, T):
                 kk = (k + j) % T
                 send(
@@ -290,70 +293,93 @@
             pl.when(cond)(body)
             send(cond, make)
 
-    def value_a(t):
-        return lambda: term[X * t + x, :G_SPLIT, :].astype(F32) + xr[t].astype(F32)
-
-    def value_b(t):
-        return lambda: term[pl.ds(X * t, X), G_SPLIT:, :].astype(F32)
-
-    def arrived_a(t):
-        xr_copy(t, o)().wait_recv()
-
-    def sum_a(s):
-        z_sum(s, value_a, arrived_a, zua, zda, sua, sda, ras, rar)
-
-    def sum_b(s):
-        z_sum(s, value_b, lambda t: None, zub, zdb, sub, sdb, rbs, rbr)
-
-    sum_b(0)
-    gw.part_b(0)
-    for s in range(Z - 1):
-        sum_a(s)
-        if s == 1:
-            gw.flush()
-        gw.part_a(s)
-        if s + 1 < Z - 1:
-            sum_b(s + 1)
-        gw.part_b(s + 1)
+    def value_a(h, t):
+        return lambda: term[h, X * t + x, :G_SPLIT, :].astype(F32) + xr[h, t].astype(F32)
+
+    def value_b(h, t):
+        return lambda: term[h, pl.ds(X * t, X), G_SPLIT:, :].astype(F32)
+
+    def arrived_a(h, t):
+        xr_copy(h, t, o)().wait_recv()
+
+    def sum_a(h, s):
+        z_sum(
+            s, lambda t: value_a(h, t), lambda t: arrived_a(h, t),
+            zua.at[h], zda.at[h], sua.at[h], sda.at[h], ras.at[h], rar.at[h],
+        )
+
+    def sum_b(h, s):
+        z_sum(
+            s, lambda t: value_b(h, t), lambda t: None,
+            zub.at[h], zdb.at[h], sub.at[h], sdb.at[h], rbs.at[h], rbr.at[h],
+        )
 
     last = Z - 2
-    sb = fxs
-    sb[...] = term[pl.ds(X * z, X), G_SPLIT:, :].astype(F32)
-    for cond, zin, base, dev in ((dn_ok, zub, 0, above), (up_ok, zdb, 3, below)):
-        def body(zin=zin, base=base, dev=dev):
-            rc(zin.at[last], zin.at[last], rbs.at[base + last], rbr.at[base + last], dev).wait_recv()
-            sb[...] += zin[last].astype(F32)
-        pl.when(cond)(body)
-    fxr[0] = sb[o].astype(BF16)
-    fx = lambda: rc(fxr.at[0], fxr.at[1], fs, fr, across)
-    send(None, fx)
-    arrived_a(z)
-    grad_t[:G_SPLIT, :] = value_a(z)()
-    for cond, zin, base, dev in ((dn_ok, zua, 0, above), (up_ok, zda, 3, below)):
-        def body(zin=zin, base=base, dev=dev):
-            rc(zin.at[last], zin.at[last], ras.at[base + last], rar.at[base + last], dev).wait_recv()
-            grad_t[:G_SPLIT, :] += zin[last].astype(F32)
-        pl.when(cond)(body)
-    fx().wait_recv()
-    gw.flush()
-    grad_t[G_SPLIT:, :] = sb[x] + fxr[1].astype(F32)
-
-    for c in moments:
-        c.wait()
-
-    for g, part in ((gn, 0), (gm, 1)):
+
+    def final_sum(h):
+        sb, ga = fxs.at[h], grad_t.at[h, pl.ds(0, G_SPLIT), :]
+        sb[...] = value_b(h, z)()
+        for cond, zin, base, dev in ((dn_ok, zub, 0, above), (up_ok, zdb, 3, below)):
+            def body(zin=zin, base=base, dev=dev):
+                slot = zin.at[h, last]
+                rc(slot, slot, rbs.at[h, base + last], rbr.at[h, base + last], dev).wait_recv()
+                sb[...] += slot[...].astype(F32)
+            pl.when(cond)(body)
+        fxr[h, 0] = sb[o].astype(BF16)
+        fx = lambda: rc(fxr.at[h, 0], fxr.at[h, 1], fs.at[h], fr.at[h], across)
+        send(None, fx)
+        arrived_a(h, z)
+        ga[...] = value_a(h, z)()
+        for cond, zin, base, dev in ((dn_ok, zua, 0, above), (up_ok, zda, 3, below)):
+            def body(zin=zin, base=base, dev=dev):
+                slot = zin.at[h, last]
+                rc(slot, slot, ras.at[h, base + last], rar.at[h, base + last], dev).wait_recv()
+                ga[...] += slot[...].astype(F32)
+            pl.when(cond)(body)
+        fx().wait_recv()
+        grad_t[h, G_SPLIT:, :] = sb[x] + fxr[h, 1].astype(F32)
+
+    def step_adam(h):
         @pl.loop(0, half // 128)
-        def _(c, part=part):
-            here = pl.ds(pl.multiple_of(part * half + c * 128, 128), 128)
+        def _(c):
+            at = pl.multiple_of(c * 128, 128)
+            here = pl.ds(h * half + at, 128)
             nm, n1, n2 = adam(
-                grad_t[:, here].T, master_ref[here, :], one_ref[here, :], two_ref[here, :]
+                grad_t[h, :, pl.ds(at, 128)].T, master_ref[here, :], one_ref[here, :], two_ref[here, :]
             )
             nm_ref[here, :] = nm
             n1_ref[here, :] = n1
             n2_ref[here, :] = n2
             nw_ref[r, here, :] = nm.astype(BF16)
 
-        g.start()
+    sum_b(0, 0)
+    gw.part_b(0)
+    sum_a(0, 0)
+    gw.part_a(0)
+    sum_b(0, 1)
+    sum_a(0, 1)
+    sum_b(1, 0)
+    sum_a(1, 0)
+    gw.part_b(1)
+    sum_b(0, 2)
+    sum_a(0, 2)
+    gw.part_a(1)
+    sum_b(1, 1)
+    sum_a(1, 1)
+    gw.part_b(2)
+    for c in moments:
+        c.wait()
+    final_sum(0)
+    step_adam(0)
+    gn.start()
+    sum_b(1, 2)
+    sum_a(1, 2)
+    gw.part_a(2)
+    gn.part_b(0)
+    gn.part_a(0)
+    final_sum(1)
+    step_adam(1)
+    gm.start()
 
     writes = []
 
@@ -365,15 +391,20 @@
     write(nm_ref, nm_hbm)
     write(n1_ref, n1_hbm)
     write(n2_ref, n2_hbm)
-    for s in range(Z - 1):
-        gn.part_a(s)
-        gm.part_a(s)
-        gn.part_b(s)
-        gm.part_b(s)
-        if s == 1:
-            gw.finish_x()
-    gn.part_b(Z - 1)
-    gm.part_b(Z - 1)
+    gw.part_b(3)
+    gn.part_b(1)
+    gn.part_a(1)
+    gm.part_b(0)
+    gw.finish_x()
+    gm.part_a(0)
+    gn.part_b(2)
+    gn.part_a(2)
+    gm.part_b(1)
+    gm.part_a(1)
+    gn.part_b(3)
+    gm.part_b(2)
+    gm.part_a(2)
+    gm.part_b(3)
 
     wx[k] = w_buf[pl.ds(X * k, X)]
     for j in range(1, T):
@@ -413,23 +444,27 @@
 
 
 def place(*refs):
-    srcs, dsts, sems = refs[:5], refs[5:10], refs[10]
-    copies = []
-    for src, dst in zip(srcs, dsts):
+    srcs, dsts, held, sems = refs[:5], refs[5:10], refs[10:15], refs[15]
+    into, out = [], []
+    for src, dst, buf in zip(srcs, dsts, held):
         step = src.shape[0] // PIECES
         for i in range(PIECES):
-            here = pl.ds(i * step, step)
-            copies.append(pltpu.make_async_copy(src.at[here], dst.at[here], sems.at[len(copies)]))
-    for c in copies:
+            here, j = pl.ds(i * step, step), len(into)
+            into.append(pltpu.make_async_copy(src.at[here], buf.at[here], sems.at[0, j]))
+            out.append(pltpu.make_async_copy(buf.at[here], dst.at[here], sems.at[1, j]))
+    for c in into:
         c.start()
-    for c in copies:
+    for c, d in zip(into, out):
         c.wait()
+        d.start()
+    for d in out:
+        d.wait()
 
 
 def local_kernel(inputs, pre_act, grad_hidden, master, moment_one, moment_two):
     tok, hid = pre_act.shape
     rows = master.shape[0]
-    n = Z * X
+    n, half = Z * X, rows // 2
     gb = hid - G_SPLIT
     vmem = pl.BlockSpec(memory_space=pltpu.VMEM)
     dma = pltpu.SemaphoreType.DMA
@@ -454,19 +489,19 @@
             pltpu.VMEM((T, X, rows, hid), BF16),
             pltpu.VMEM((T, tok, hid), BF16),
             pltpu.VMEM((hid, tok), BF16),
-            pltpu.VMEM((n, hid, rows), BF16),
-            pltpu.VMEM((Z, G_SPLIT, rows), BF16),
-            *[pltpu.VMEM((Z - 1, G_SPLIT, rows), BF16)] * 4,
-            *[pltpu.VMEM((Z - 1, X, gb, rows), BF16)] * 4,
-            pltpu.VMEM((X, gb, rows), F32),
-            pltpu.VMEM((2, gb, rows), BF16),
-            pltpu.VMEM((hid, rows), F32),
+            pltpu.VMEM((2, n, hid, half), BF16),
+            pltpu.VMEM((2, Z, G_SPLIT, half), BF16),
+            *[pltpu.VMEM((2, Z - 1, G_SPLIT, half), BF16)] * 4,
+            *[pltpu.VMEM((2, Z - 1, X, gb, half), BF16)] * 4,
+            pltpu.VMEM((2, X, gb, half), F32),
+            pltpu.VMEM((2, 2, gb, half), BF16),
+            pltpu.VMEM((2, hid, half), F32),
             dma((tok // 256 + Z + 3,)), dma((2,)), dma((n,)), dma((T - 1,)), dma((T - 1,)),
             dma((Z * X * 2,)), dma((T * X * 2,)),
             dma((2, 17)), dma((2, 17)), dma((2, 17)),
-            dma((Z,)), dma((Z,)),
-            dma((6,)), dma((6,)), dma((6,)), dma((6,)),
-            dma(()), dma(()),
+            dma((2, Z)), dma((2, Z)),
+            dma((2, 6)), dma((2, 6)), dma((2, 6)), dma((2, 6)),
+            dma((2,)), dma((2,)),
         ],
         compiler_params=pltpu.CompilerParams(
             collective_id=0, has_side_effects=True, vmem_limit_bytes=60 * 1024 * 1024
@@ -480,7 +515,7 @@
         out_shape=tuple(jax.ShapeDtypeStruct(a.shape, a.dtype) for a in out),
         in_specs=[hbm] * 5,
         out_specs=[hbm] * 5,
-        scratch_shapes=[dma((5 * PIECES,))],
+        scratch_shapes=[*[pltpu.VMEM(a.shape, a.dtype) for a in out], dma((2, 5 * PIECES))],
         compiler_params=pltpu.CompilerParams(vmem_limit_bytes=60 * 1024 * 1024),
         cost_estimate=pl.CostEstimate(flops=0, bytes_accessed=2 * 9 * 2**20, transcendentals=0),
     )(*out)

time: 369 us -> 110 us (0.30)
  Pallas kernels: 368 us -> 109 us
    pallas_call x1, Pallas kernels: 263 us -> 6.72 us  [local_kernel(): pl.pallas_call(place, out_shape=tuple((jax.ShapeDtypeStruct(a.shape, a.dt...]
where the time goes in v4:
time: 110 us
  Pallas kernels  109 us (99%)
    pallas_call x1, Pallas kernels, local_kernel(): pl.pallas_call(kernel, out_shape=(jax.ShapeDtypeStruct((tok, rows * X), B...  103 us
    pallas_call x1, Pallas kernels, local_kernel(): pl.pallas_call(place, out_shape=tuple((jax.ShapeDtypeStruct(a.shape, a.dt...  6.72 us

profile of v4, /device:TPU:0, one launch (start us, length us, event | category | flops | bytes accessed | tf_op | source)
XLA Modules:
  0.0 110.1 jit_solution(11892474994290415652)
XLA Ops:
  0.6 102.7 %shard_map.101 = (bf16[1024,1536]{1,0:T(8,128)(2,1)}, f32[768,256]{1,0:T(8,128)}, f32[768,256]{1,0:T(8,128)}, f32[768,256]{1,0:T(8,128)}, bf16[8,768,256]{2,1,0:T(8,128)(2,1)}) custom-call(bf16[1024,6144]{1,0:T(8,128)(2,1)} %in_hbm.1, bf16[1024,256]{1,0:T(8,128)(2,1)} %pre_ref.1, bf16[1024,256]{1,0:T(8,128)(2,1)} %hid_ref.1, f32[768,256]{1,0:T(8,128)} %master_ref.1, ...), custom_call_target="tpu_custom_call" | custom-call | flops 6442450944 | bytes 25165824 | tf_op jit(solution)/shard_map/pallas_call | solution.py:472
  103.4 6.7 %shard_map.102 = (bf16[1024,1536]{1,0:T(8,128)(2,1)}, f32[768,256]{1,0:T(8,128)}, f32[768,256]{1,0:T(8,128)}, f32[768,256]{1,0:T(8,128)}, bf16[8,768,256]{2,1,0:T(8,128)(2,1)}) custom-call(bf16[1024,1536]{1,0:T(8,128)(2,1)} %get-tuple-element.15.refs_0_, f32[768,256]{1,0:T(8,128)} %get-tuple-element.16.refs_1_, f32[768,256]{1,0:T(8,128)} %get-tuple-element.17.refs_2_, ...), custom_call_target="tpu_custom_call" | custom-call | bytes 18874368 | tf_op jit(solution)/shard_map/pallas_call | solution.py:513

commit v5 on v4

--- a/solution.py
+++ b/solution.py
@@ -237,34 +237,15 @@
         if h == 0:
             fetch(j).wait()
 
-        @pl.loop(0, half // 128)
-        def _(c):
-            at = pl.multiple_of(c * 128, 128)
-            cols = pl.ds(h * half + at, 128)
-            t = jnp.dot(act_t[...], xin[j, :, cols], preferred_element_type=F32)
-            scale = (jnp.max(jnp.abs(t), axis=0, keepdims=True) + 1e-06) / 127.0
-            codes = jnp.clip(t / scale, -127.0, 127.0).astype(BF16)
-            term[h, blk, :, pl.ds(at, 128)] = (codes.astype(F32) * scale).astype(BF16)
+        t = jnp.dot(act_t[...], xin[j, :, pl.ds(h * half, half)], preferred_element_type=F32)
+        scale = (jnp.max(jnp.abs(t), axis=0, keepdims=True) + 1e-06) / 127.0
+        codes = jnp.clip(t * (1.0 / scale), -127.0, 127.0).astype(BF16)
+        term[h, blk] = (codes.astype(F32) * scale).astype(BF16)
 
     def xr_copy(h, t, own):
         return lambda: rc(
             term.at[h, X * t + own, pl.ds(0, G_SPLIT), :], xr.at[h, t], rxs.at[h, t], rxr.at[h, t], across
         )
-
-    for h in range(2):
-        for i in range(Z):
-            make_term(h, 2 * i)
-            send(None, xr_copy(h, order[i], o))
-            make_term(h, 2 * i + 1)
-        if h == 0:
-            for j in range(1, T):
-                kk = (k + j) % T
-                send(
-                    None,
-                    lambda kk=kk, j=j: rc(
-                        act.at[k], act.at[k], act_s.at[j - 1], act_r.at[j - 1], {"tensor": kk}
-                    ),
-                )
 
     def z_sum(s, value, arrived, zu, zd, su, sd, ssem, rsem):
         tu, td = z + 3 - s, z - 3 + s
@@ -352,15 +333,34 @@
             n2_ref[here, :] = n2
             nw_ref[r, here, :] = nm.astype(BF16)
 
+    def terms(h, i):
+        make_term(h, 2 * i)
+        send(None, xr_copy(h, order[i], o))
+        make_term(h, 2 * i + 1)
+
+    terms(0, 0)
+    gw.part_b(0)
+    terms(0, 1)
+    terms(0, 2)
+    gw.part_a(0)
+    terms(0, 3)
     sum_b(0, 0)
-    gw.part_b(0)
     sum_a(0, 0)
-    gw.part_a(0)
+    for j in range(1, T):
+        kk = (k + j) % T
+        send(
+            None,
+            lambda kk=kk, j=j: rc(act.at[k], act.at[k], act_s.at[j - 1], act_r.at[j - 1], {"tensor": kk}),
+        )
+    terms(1, 0)
+    terms(1, 1)
     sum_b(0, 1)
+    gw.part_b(1)
+    terms(1, 2)
     sum_a(0, 1)
+    terms(1, 3)
     sum_b(1, 0)
     sum_a(1, 0)
-    gw.part_b(1)
     sum_b(0, 2)
     sum_a(0, 2)
     gw.part_a(1)

time: 110 us -> 105 us (0.955)
  Pallas kernels: 109 us -> 104 us
    pallas_call x1, Pallas kernels: 103 us -> 97.2 us  [local_kernel(): pl.pallas_call(kernel, out_shape=(jax.ShapeDtypeStruct((tok, rows * X), B...]
where the time goes in v5:
time: 105 us
  Pallas kernels  104 us (99%)
    pallas_call x1, Pallas kernels, local_kernel(): pl.pallas_call(kernel, out_shape=(jax.ShapeDtypeStruct((tok, rows * X), B...  97.2 us
    pallas_call x1, Pallas kernels, local_kernel(): pl.pallas_call(place, out_shape=tuple((jax.ShapeDtypeStruct(a.shape, a.dt...  6.72 us

profile of v5, /device:TPU:0, one launch (start us, length us, event | category | flops | bytes accessed | tf_op | source)
XLA Modules:
  0.0 104.7 jit_solution(7535522366301943963)
XLA Ops:
  0.6 97.2 %shard_map.101 = (bf16[1024,1536]{1,0:T(8,128)(2,1)}, f32[768,256]{1,0:T(8,128)}, f32[768,256]{1,0:T(8,128)}, f32[768,256]{1,0:T(8,128)}, bf16[8,768,256]{2,1,0:T(8,128)(2,1)}) custom-call(bf16[1024,6144]{1,0:T(8,128)(2,1)} %in_hbm.1, bf16[1024,256]{1,0:T(8,128)(2,1)} %pre_ref.1, bf16[1024,256]{1,0:T(8,128)(2,1)} %hid_ref.1, f32[768,256]{1,0:T(8,128)} %master_ref.1, ...), custom_call_target="tpu_custom_call" | custom-call | flops 6442450944 | bytes 25165824 | tf_op jit(solution)/shard_map/pallas_call | solution.py:472
  97.8 6.7 %shard_map.102 = (bf16[1024,1536]{1,0:T(8,128)(2,1)}, f32[768,256]{1,0:T(8,128)}, f32[768,256]{1,0:T(8,128)}, f32[768,256]{1,0:T(8,128)}, bf16[8,768,256]{2,1,0:T(8,128)(2,1)}) custom-call(bf16[1024,1536]{1,0:T(8,128)(2,1)} %get-tuple-element.15.refs_0_, f32[768,256]{1,0:T(8,128)} %get-tuple-element.16.refs_1_, f32[768,256]{1,0:T(8,128)} %get-tuple-element.17.refs_2_, ...), custom_call_target="tpu_custom_call" | custom-call | bytes 18874368 | tf_op jit(solution)/shard_map/pallas_call | solution.py:513

commit v6 on v5

--- a/solution.py
+++ b/solution.py
@@ -11,7 +11,7 @@
 QBLOCK = 256
 ADAM_STEP = 10
 Z, X, T = 4, 2, 4
-W_SPLIT = 464
+W_SPLIT = 544
 G_SPLIT = 160
 N_SPLIT = 352
 PIECES = 4

time: 105 us -> 108 us (1.029)
  Pallas kernels: 104 us -> 107 us
    pallas_call x1, Pallas kernels: 97.2 us -> 99.8 us  [local_kernel(): pl.pallas_call(kernel, out_shape=(jax.ShapeDtypeStruct((tok, rows * X), B...]
where the time goes in v6:
time: 108 us; the launch traced here: 107 us
  Pallas kernels  107 us (99%)
    pallas_call x1, Pallas kernels, local_kernel(): pl.pallas_call(kernel, out_shape=(jax.ShapeDtypeStruct((tok, rows * X), B...  99.8 us
    pallas_call x1, Pallas kernels, local_kernel(): pl.pallas_call(place, out_shape=tuple((jax.ShapeDtypeStruct(a.shape, a.dt...  6.72 us

profile of v6, /device:TPU:0, one launch (start us, length us, event | category | flops | bytes accessed | tf_op | source)
XLA Modules:
  0.0 107.4 jit_solution(346105905031122334)
XLA Ops:
  0.6 99.8 %shard_map.101 = (bf16[1024,1536]{1,0:T(8,128)(2,1)}, f32[768,256]{1,0:T(8,128)}, f32[768,256]{1,0:T(8,128)}, f32[768,256]{1,0:T(8,128)}, bf16[8,768,256]{2,1,0:T(8,128)(2,1)}) custom-call(bf16[1024,6144]{1,0:T(8,128)(2,1)} %in_hbm.1, bf16[1024,256]{1,0:T(8,128)(2,1)} %pre_ref.1, bf16[1024,256]{1,0:T(8,128)(2,1)} %hid_ref.1, f32[768,256]{1,0:T(8,128)} %master_ref.1, ...), custom_call_target="tpu_custom_call" | custom-call | flops 6442450944 | bytes 25165824 | tf_op jit(solution)/shard_map/pallas_call | solution.py:472
  100.5 6.7 %shard_map.102 = (bf16[1024,1536]{1,0:T(8,128)(2,1)}, f32[768,256]{1,0:T(8,128)}, f32[768,256]{1,0:T(8,128)}, f32[768,256]{1,0:T(8,128)}, bf16[8,768,256]{2,1,0:T(8,128)(2,1)}) custom-call(bf16[1024,1536]{1,0:T(8,128)(2,1)} %get-tuple-element.15.refs_0_, f32[768,256]{1,0:T(8,128)} %get-tuple-element.16.refs_1_, f32[768,256]{1,0:T(8,128)} %get-tuple-element.17.refs_2_, ...), custom_call_target="tpu_custom_call" | custom-call | bytes 18874368 | tf_op jit(solution)/shard_map/pallas_call | solution.py:513
